TPU v7x, 256 devices: a whole 4x4x8 slice. The times are simulated.
256 devices in a mesh: gx: 8 (over x, core), gy: 32 (over z, y).
Axes of the slice: x: 4, y: 4, z: 8, core: 2. Of those that a mesh axis runs over, the one named last changes fastest.
Arguments:
- state_field: float32 [256, 512, 16, 256], P('gx', 'gy'), may hold values from -80 to 80
- start_basis: float32 [256, 32], replicated, may hold values from -6 to 6
Outputs:
- core_tensor: float32 [256, 512, 512], P('gx', 'gy')
- z_factor: float32 [256, 32], replicated
- x_triangle: float32 [256, 256], replicated
All inputs are finite; a program needn't handle non-finite values.
Results may differ from a plain program's by a relative error of at most 0.0003.
Values sent between devices are 32-bit elements; how exact they have to be, the bound alone decides.
A program may use at most 64 MiB of HBM per device.

v0:
```python
import jax
import jax.numpy as jnp
from jax import lax
from jax.sharding import PartitionSpec as P

ITERS = 3
precise = lax.Precision.HIGHEST


def orthonormal(image):
    for repeat in range(2):
        inner_gram = jnp.dot(image.T, image, precision=precise, preferred_element_type=jnp.float32)
        lower_factor = jnp.linalg.cholesky(inner_gram)
        image = lax.linalg.triangular_solve(
            lower_factor, image, left_side=False, lower=True, transpose_a=True
        )
    return image


def local(state_field, start_basis):
    x_cells, y_cells, species, z_cells = state_field.shape
    unfolded = state_field.reshape(x_cells * y_cells * species, z_cells)
    local_gram = lax.dot_general(
        unfolded,
        unfolded,
        (((0,), (0,)), ((), ())),
        precision=precise,
        preferred_element_type=jnp.float32,
    )
    z_basis = start_basis
    gram_z = lax.psum(local_gram, ("gx", "gy"))
    for iteration in range(ITERS):
        z_basis = orthonormal(
            jnp.dot(gram_z, z_basis, precision=precise, preferred_element_type=jnp.float32)
        )
    rank_kept = z_basis.shape[1]
    core_rows = jnp.dot(unfolded, z_basis, precision=precise, preferred_element_type=jnp.float32)
    core_tensor = core_rows.reshape(x_cells, y_cells, species * rank_kept)
    x_total = x_cells * lax.axis_size("gx")
    regrouped = lax.all_to_all(core_tensor, "gx", split_axis=2, concat_axis=0, tiled=True)
    x_rows = regrouped.reshape(x_total, -1)
    local_xgram = jnp.dot(x_rows, x_rows.T, precision=precise, preferred_element_type=jnp.float32)
    gram_x = lax.psum(local_xgram, ("gx", "gy"))
    column_count = y_cells * lax.axis_size("gy") * species * rank_kept
    x_triangle = jnp.linalg.cholesky(gram_x).T / jnp.sqrt(jnp.float32(column_count))
    return (core_tensor, z_basis, x_triangle)


def solution(mesh):
    return jax.shard_map(
        local,
        mesh=mesh,
        in_specs=(P("gx", "gy", None, None), P()),
        out_specs=(P("gx", "gy", None), P(), P()),
        check_vma=False,
    )
```

profile of v0, /device:TPU:2, one launch (start us, length us, event | category | flops | bytes accessed | tf_op | source)
XLA Modules:
  0.0 675.3 jit_solution(2987790697292606197)
XLA Ops:
  7.2 17.8 %convolution_bitcast_fusion.1 = f32[256,256]{1,0:T(8,128)} fusion(f32[32,16,16,256]{3,2,1,0:T(8,128)} %param.5), kind=kOutput, calls=%fused_computation.1 | convolution fusion | flops 6442450944 | bytes 8650752 | tf_op jit(solution)/shard_map/dot_general | solution.py:23
  25.3 253.2 %all-reduce.4.cloned.1.call-done = f32[256,256]{1,0:T(8,128)} async-done(((f32[256,256]{1,0:T(8,128)}), f32[256,256]{1,0:T(8,128)}) %all-reduce.4.cloned.1.call-update) | async-done | bytes 262160 | tf_op jit(solution)/shard_map/psum | solution.py:31
  278.4 1.3 fusion.32
  280.0 2.9 cholesky.222
  284.2 2.4 custom-call.22
  287.2 2.9 cholesky.233
  291.4 2.4 custom-call.23
  294.1 1.3 fusion.35
  295.7 2.9 cholesky.244
  299.9 2.4 custom-call.24
  302.9 2.9 cholesky.255
  307.1 2.4 custom-call.25
  309.8 1.3 fusion.38
  311.3 2.9 cholesky.266
  315.6 2.4 custom-call.26
  318.5 2.9 cholesky.277
  322.8 2.4 custom-call.27
  325.5 9.9 %convolution_bitcast_fusion = f32[8192,32]{0,1:T(8,128)S(1)} fusion(f32[256,32]{0,1:T(8,128)S(1)} %convolution_bitcast_fusion.2, f32[8192,256]{1,0:T(8,128)} %bitcast.127), kind=kOutput, calls=%fused_computation | convolution fusion | flops 805306368 | bytes 9469952 | tf_op jit(solution)/shard_map/dot_general | solution.py:37
  335.4 2.6 copy.47
  338.0 3.5 reshape.41
  341.6 3.8 copy.48
  345.4 3.9 reshape.66
  349.3 19.2 %all_to_all.15 = f32[8,1,32768]{2,1,0:T(1,128)S(1)} all-to-all(f32[8,1,32768]{2,1,0:T(1,128)S(1)} %reshape.66), channel_id=1, replica_groups=mesh['gx'=8,'gy'=32] {'gx'}, dimensions={0} | all-to-all | bytes 2097152 | tf_op jit(solution)/shard_map/all_to_all | solution.py:40
  369.1 3.1 reduce.16
  372.2 3.3 reshape.67
  375.5 3.6 copy.49
  379.7 1.7 fusion.41
  381.5 248.1 %all-reduce.6.cloned.1.call-done = f32[256,256]{0,1:T(8,128)} async-done(((f32[256,256]{0,1:T(8,128)}), f32[256,256]{0,1:T(8,128)}) %all-reduce.6.cloned.1.call-update) | async-done | bytes 262160 | tf_op jit(solution)/shard_map/psum | solution.py:43
  629.6 1.1 copy.51
  631.7 11.7 %cholesky.77 = f32[128,128]{1,0:T(8,128)S(1)} custom-call(f32[128,128]{1,0:T(8,128)S(1)} %cholesky.286), custom_call_target="Cholesky" | custom-call | tf_op jit(solution)/shard_map/jit(cholesky)/cholesky | solution.py:45
  643.4 9.8 %custom-call.16 = f32[1,128,128]{1,2,0:T(8,128)S(1)} custom-call(f32[1,128,128]{2,1,0:T(8,128)S(1)} %get-tuple-element.20), custom_call_target="InvertDiagBlocksLowerTriangular" | custom-call | tf_op jit(solution)/shard_map/jit(cholesky)/cholesky | solution.py:45
  653.8 11.7 %cholesky.132 = f32[128,128]{1,0:T(8,128)S(1)} custom-call(f32[128,128]{1,0:T(8,128)S(1)} %convolution_subtract_fusion), custom_call_target="Cholesky" | custom-call | tf_op jit(solution)/shard_map/jit(cholesky)/cholesky | solution.py:45
  (64 shorter events, 15.4 us)
Async XLA Ops:
  7.2 271.3 %copy-start = (f32[256,32]{0,1:T(8,128)S(1)}, f32[256,32]{0,1:T(8,128)}, u32[]{:S(2)}) copy-start(f32[256,32]{0,1:T(8,128)} %param.6) | copy-start | bytes 98308
  7.2 271.2 %all-reduce.4.cloned.1.call-start = ((), (), s32[]{:S(2)}) async-start(), calls=%async_computation.1 | async-start | bytes 524288 | tf_op jit(solution)/shard_map/psum | solution.py:31
  25.0 604.6 %all-reduce.6.cloned.1.call-start = ((), (), s32[]{:S(2)}) async-start(), calls=%async_computation.2 | async-start | bytes 524288 | tf_op jit(solution)/shard_map/psum | solution.py:43
  325.5 16.1 %copy-start.2 = (f32[256,32]{0,1:T(8,128)}, f32[256,32]{0,1:T(8,128)S(1)}, u32[]{:S(2)}) copy-start(f32[256,32]{0,1:T(8,128)S(1)} %convolution_bitcast_fusion.2) | copy-start | bytes 98308
  341.6 34.0 %copy-start.1 = (f32[32,16,512]{2,1,0:T(8,128)}, f32[32,16,512]{2,1,0:T(8,128)S(1)}, u32[]{:S(2)}) copy-start(f32[32,16,512]{2,1,0:T(8,128)S(1)} %reshape.41) | copy-start | bytes 3145732
Sparse Core Ops, SparseCore 0:
  25.2 253.2 all-reduce.3
  381.6 247.9 all-reduce.5
where the time goes:
time: 676 us; the launch traced here: 675 us
  waiting for transfers between devices  501 us (74%)
  other arithmetic  78.3 us (12%)
  matrix products  36.2 us (5%)
  local copies, waits for them, and re-layouts  24.3 us (4%)
  blocking collectives  19.2 us (3%)
  between operations  15.7 us (2%)
    psum x1, waiting for transfers between devices, local(): gram_z = lax.psum(local_gram, ('gx', 'gy'))  253 us
    psum x1, waiting for transfers between devices, local(): gram_x = lax.psum(local_xgram, ('gx', 'gy'))  248 us
    another operation x6, other arithmetic, local(): jnp.linalg.cholesky(gram_x).T / jnp.sqrt(jnp.float32(column_count))  34 us
    another operation x18, other arithmetic, orthonormal(): lower_factor = jnp.linalg.cholesky(inner_gram)  21.6 us
    all_to_all x1, blocking collectives, local(): lax.all_to_all(core_tensor, 'gx', split_axis=2, concat_axis=0, tiled=True)  19.2 us
    another operation x12, other arithmetic, orthonormal(): lax.linalg.triangular_solve(lower_factor, image, left_side=False, lower=T...  18.5 us
    dot_general x1, matrix products, local(): lax.dot_general(unfolded, unfolded, (((0,), (0,)), ((), ())), precision=p...  17.8 us
  transfers between devices with their start and end apart: 2, of which 2 were waited for; matrix products, arithmetic and copies ran while one was open for 0% of the time, Pallas kernels for 0%

commit v1 on v0

--- a/solution.py
+++ b/solution.py
@@ -1,3 +1,4 @@
+import functools
 import jax
 import jax.numpy as jnp
 from jax import lax
@@ -5,6 +6,29 @@
 
 ITERS = 3
 precise = lax.Precision.HIGHEST
+
+
+def pairs_all_turn(inner_x, axis_tag):
+    opened = lax.axis_size(axis_tag)
+    tall = lax.axis_index(axis_tag)
+    block_next, res = (opened, tall)
+    mid_arr = inner_x.shape[2] // block_next
+    current_value = list(inner_x.shape)
+    current_value[2] = mid_arr
+    fresh = current_value[0]
+    current_value[0] = fresh * block_next
+    w_next = jnp.zeros(current_value, inner_x.dtype)
+    for idx in range(block_next):
+        placed = lax.dynamic_slice_in_dim(inner_x, (res ^ idx) * mid_arr, mid_arr, axis=2)
+        if idx:
+            placed = lax.ppermute(
+                placed, axis_name=axis_tag, perm=[(u, u ^ idx) for u in range(block_next)]
+            )
+        w_next = lax.dynamic_update_slice_in_dim(w_next, placed, (res ^ idx) * fresh, axis=0)
+    return w_next
+
+
+fix_members_all = functools.partial(pairs_all_turn, axis_tag="gx")
 
 
 def orthonormal(image):
@@ -37,7 +61,7 @@
     core_rows = jnp.dot(unfolded, z_basis, precision=precise, preferred_element_type=jnp.float32)
     core_tensor = core_rows.reshape(x_cells, y_cells, species * rank_kept)
     x_total = x_cells * lax.axis_size("gx")
-    regrouped = lax.all_to_all(core_tensor, "gx", split_axis=2, concat_axis=0, tiled=True)
+    regrouped = fix_members_all(core_tensor)
     x_rows = regrouped.reshape(x_total, -1)
     local_xgram = jnp.dot(x_rows, x_rows.T, precision=precise, preferred_element_type=jnp.float32)
     gram_x = lax.psum(local_xgram, ("gx", "gy"))

time: 676 us -> 690 us (1.021)
  local copies, waits for them, and re-layouts: 24.3 us -> 43.6 us
  blocking collectives: 19.2 us -> 0 us
  starting transfers between devices: 0.26 us -> 7.58 us
    dynamic_update_slice x0 -> x8, local copies, waits for them, and re-layouts: none -> 24.9 us  [pairs_all_turn(): lax.dynamic_update_slice_in_dim(w_next, placed, (res ^ idx) * fresh, axis=0)]
    all_to_all x1 -> x0, blocking collectives: 19.2 us -> none  [local(): lax.all_to_all(core_tensor, 'gx', split_axis=2, concat_axis=0, tiled=True)]
    ppermute x0 -> x7, local copies, waits for them, and re-layouts: none -> 8.15 us  [pairs_all_turn(): lax.ppermute(placed, axis_name=axis_tag, perm=[(u, u ^ idx) for u in rang...]
    ppermute x0 -> x7, starting transfers between devices: none -> 7.04 us  [pairs_all_turn(): lax.ppermute(placed, axis_name=axis_tag, perm=[(u, u ^ idx) for u in rang...]
    unnamed x9 -> x11, local copies, waits for them, and re-layouts: 8.08 us -> 1.15 us
  transfers between devices with their start and end apart: 2 -> 9, of which waited for: 2 -> 3; matrix products, arithmetic and copies ran while one was open for 0% -> 4% of each run, Pallas kernels for 0% -> 0%
where the time goes in v1:
time: 690 us; the launch traced here: 684 us
  waiting for transfers between devices  505 us (73%)
  other arithmetic  75.2 us (11%)
  local copies, waits for them, and re-layouts  43.6 us (6%)
  matrix products  37 us (5%)
  between operations  16.1 us (2%)
  starting transfers between devices  7.58 us (1%)
    psum x1, waiting for transfers between devices, local(): gram_z = lax.psum(local_gram, ('gx', 'gy'))  253 us
    psum x1, waiting for transfers between devices, local(): gram_x = lax.psum(local_xgram, ('gx', 'gy'))  249 us
    another operation x6, other arithmetic, local(): jnp.linalg.cholesky(gram_x).T / jnp.sqrt(jnp.float32(column_count))  34 us
    dynamic_update_slice x8, local copies, waits for them, and re-layouts, pairs_all_turn(): lax.dynamic_update_slice_in_dim(w_next, placed, (res ^ idx) * fresh, axis=0)  24.9 us
    another operation x18, other arithmetic, orthonormal(): lower_factor = jnp.linalg.cholesky(inner_gram)  21.6 us
    another operation x12, other arithmetic, orthonormal(): lax.linalg.triangular_solve(lower_factor, image, left_side=False, lower=T...  18.5 us
    dot_general x1, matrix products, local(): lax.dot_general(unfolded, unfolded, (((0,), (0,)), ((), ())), precision=p...  17.8 us
  transfers between devices with their start and end apart: 9, of which 3 were waited for; matrix products, arithmetic and copies ran while one was open for 4% of the time, Pallas kernels for 0%

profile of v1, /device:TPU:2, one launch (start us, length us, event | category | flops | bytes accessed | tf_op | source)
XLA Modules:
  0.0 684.1 jit_solution(1794165583123369553)
XLA Ops:
  7.2 17.8 %convolution_bitcast_fusion.2 = f32[256,256]{1,0:T(8,128)} fusion(f32[32,16,16,256]{3,2,1,0:T(8,128)} %param.5), kind=kOutput, calls=%fused_computation.2 | convolution fusion | flops 6442450944 | bytes 8650752 | tf_op jit(solution)/shard_map/dot_general | solution.py:47
  25.6 252.8 %all-reduce.4.cloned.1.call-done = f32[256,256]{1,0:T(8,128)} async-done(((f32[256,256]{1,0:T(8,128)}), f32[256,256]{1,0:T(8,128)}) %all-reduce.4.cloned.1.call-update) | async-done | bytes 262160 | tf_op jit(solution)/shard_map/psum | solution.py:55
  280.0 2.9 cholesky.222
  284.2 2.4 custom-call.22
  287.2 2.9 cholesky.233
  291.4 2.4 custom-call.23
  295.7 2.9 cholesky.244
  299.9 2.4 custom-call.24
  302.9 2.9 cholesky.255
  307.1 2.4 custom-call.25
  311.3 2.9 cholesky.266
  315.6 2.4 custom-call.26
  318.5 2.9 cholesky.277
  322.8 2.4 custom-call.27
  325.5 9.9 %convolution_bitcast_fusion = f32[8192,32]{0,1:T(8,128)S(1)} fusion(f32[256,32]{0,1:T(8,128)S(1)} %convolution_bitcast_fusion.3, f32[8192,256]{1,0:T(8,128)} %bitcast.120), kind=kOutput, calls=%fused_computation | convolution fusion | flops 805306368 | bytes 9469952 | tf_op jit(solution)/shard_map/dot_general | solution.py:61
  335.4 2.6 copy.32
  338.0 3.5 reshape.38
  343.4 1.5 collective-permute-start.2
  344.8 2.2 collective-permute-start.3
  348.1 1.5 collective-permute-start.5
  349.6 2.5 collective-permute-done.1
  353.1 3.9 dynamic_update_slice.24
  358.2 3.9 dynamic_update_slice.25
  365.7 3.9 dynamic_update_slice.27
  370.8 3.6 dynamic_update_slice.28
  375.5 3.6 dynamic_update_slice.29
  382.5 3.8 dynamic_update_slice.31
  386.3 2.5 convolution_bitcast_fusion.1
  388.9 249.3 %all-reduce.6.cloned.1.call-done = f32[256,256]{0,1:T(8,128)} async-done(((f32[256,256]{0,1:T(8,128)}), f32[256,256]{0,1:T(8,128)}) %all-reduce.6.cloned.1.call-update) | async-done | bytes 262160 | tf_op jit(solution)/shard_map/psum | solution.py:67
  640.3 11.7 %cholesky.77 = f32[128,128]{1,0:T(8,128)S(1)} custom-call(f32[128,128]{1,0:T(8,128)S(1)} %cholesky.286), custom_call_target="Cholesky" | custom-call | tf_op jit(solution)/shard_map/jit(cholesky)/cholesky | solution.py:69
  652.0 9.8 %custom-call.16 = f32[1,128,128]{1,2,0:T(8,128)S(1)} custom-call(f32[1,128,128]{2,1,0:T(8,128)S(1)} %get-tuple-element.22), custom_call_target="InvertDiagBlocksLowerTriangular" | custom-call | tf_op jit(solution)/shard_map/jit(cholesky)/cholesky | solution.py:69
  662.3 11.7 %cholesky.132 = f32[128,128]{1,0:T(8,128)S(1)} custom-call(f32[128,128]{1,0:T(8,128)S(1)} %convolution_subtract_fusion), custom_call_target="Cholesky" | custom-call | tf_op jit(solution)/shard_map/jit(cholesky)/cholesky | solution.py:69
  (92 shorter events, 34.0 us)
Async XLA Ops:
  7.2 271.3 %copy-start = (f32[256,32]{0,1:T(8,128)S(1)}, f32[256,32]{0,1:T(8,128)}, u32[]{:S(2)}) copy-start(f32[256,32]{0,1:T(8,128)} %param.6) | copy-start | bytes 98308
  7.2 271.2 %all-reduce.4.cloned.1.call-start = ((), (), s32[]{:S(2)}) async-start(), calls=%async_computation | async-start | bytes 524288 | tf_op jit(solution)/shard_map/psum | solution.py:55
  25.0 613.1 %all-reduce.6.cloned.1.call-start = ((), (), s32[]{:S(2)}) async-start(), calls=%async_computation.1 | async-start | bytes 524288 | tf_op jit(solution)/shard_map/psum | solution.py:67
  325.5 16.1 %copy-start.4 = (f32[256,32]{0,1:T(8,128)}, f32[256,32]{0,1:T(8,128)S(1)}, u32[]{:S(2)}) copy-start(f32[256,32]{0,1:T(8,128)S(1)} %convolution_bitcast_fusion.3) | copy-start | bytes 98308
  341.6 38.7 %copy-start.1 = (f32[32,16,512]{2,1,0:T(8,128)}, f32[32,16,512]{2,1,0:T(8,128)S(1)}, u32[]{:S(2)}) copy-start(f32[32,16,512]{2,1,0:T(8,128)S(1)} %reshape.38) | copy-start | bytes 3145732
  343.0 5.2 collective-permute-start
  343.0 9.1 %collective-permute-start.1 = (f32[32,16,64]{2,1,0:T(8,128)S(1)}, f32[32,16,64]{2,1,0:T(8,128)S(1)}, u32[]{:S(2)}, u32[]{:S(2)}) collective-permute-start(f32[32,16,64]{2,1,0:T(8,128)S(1)} %get-tuple-element.16), channel_id=1, source_target_pairs={{0,64},{32,96},{64,0},{96,32},{128,192},{160,224},{192,128},{224,1... | collective-permute-start | bytes 393224 | tf_op jit(solution)/shard_map/ppermute | solution.py:24
  343.4 21.2 %collective-permute-start.2 = (f32[32,16,64]{2,1,0:T(8,128)}, f32[32,16,64]{2,1,0:T(8,128)}, u32[]{:S(2)}, u32[]{:S(2)}) collective-permute-start(f32[32,16,64]{2,1,0:T(8,128)} %get-tuple-element.15), channel_id=1, source_target_pairs={{0,96},{32,64},{64,32},{96,0},{128,224},{160,192},{192,160},{224,1... | collective-permute-start | bytes 393224 | tf_op jit(solution)/shard_map/ppermute | solution.py:24
  344.8 24.7 %collective-permute-start.3 = (f32[32,16,64]{2,1,0:T(8,128)}, f32[32,16,64]{2,1,0:T(8,128)}, u32[]{:S(2)}, u32[]{:S(2)}) collective-permute-start(f32[32,16,64]{2,1,0:T(8,128)} %get-tuple-element.14), channel_id=1, source_target_pairs={{0,128},{32,160},{64,192},{96,224},{128,0},{160,32},{192,64},{224,... | collective-permute-start | bytes 393224 | tf_op jit(solution)/shard_map/ppermute | solution.py:24
  347.1 27.3 %collective-permute-start.4 = (f32[32,16,64]{2,1,0:T(8,128)S(1)}, f32[32,16,64]{2,1,0:T(8,128)}, u32[]{:S(2)}, u32[]{:S(2)}) collective-permute-start(f32[32,16,64]{2,1,0:T(8,128)S(1)} %get-tuple-element.13), channel_id=1, source_target_pairs={{0,160},{32,128},{64,224},{96,192},{128,32},{160,0},{192,96},{224,... | collective-permute-start | bytes 393224 | tf_op jit(solution)/shard_map/ppermute | solution.py:24
  348.1 4.4 copy-start.3
  348.1 31.0 %collective-permute-start.5 = (f32[32,16,64]{2,1,0:T(8,128)S(1)}, f32[32,16,64]{2,1,0:T(8,128)}, u32[]{:S(2)}, u32[]{:S(2)}) collective-permute-start(f32[32,16,64]{2,1,0:T(8,128)S(1)} %get-tuple-element.12), channel_id=1, source_target_pairs={{0,192},{32,224},{64,128},{96,160},{128,64},{160,96},{192,0},{224,... | collective-permute-start | bytes 393224 | tf_op jit(solution)/shard_map/ppermute | solution.py:24
  352.1 0.7 copy-start.2
  352.1 29.3 %collective-permute-start.6 = (f32[32,16,64]{2,1,0:T(8,128)S(1)}, f32[32,16,64]{2,1,0:T(8,128)}, u32[]{:S(2)}, u32[]{:S(2)}) collective-permute-start(f32[32,16,64]{2,1,0:T(8,128)S(1)} %get-tuple-element.11), channel_id=1, source_target_pairs={{0,224},{32,192},{64,160},{96,128},{128,96},{160,64},{192,32},{224... | collective-permute-start | bytes 393224 | tf_op jit(solution)/shard_map/ppermute | solution.py:24
Sparse Core Ops, SparseCore 0:
  25.2 253.2 all-reduce.3
  389.0 249.1 all-reduce.5

commit v2 on v0

--- a/solution.py
+++ b/solution.py
@@ -40,7 +40,9 @@
     regrouped = lax.all_to_all(core_tensor, "gx", split_axis=2, concat_axis=0, tiled=True)
     x_rows = regrouped.reshape(x_total, -1)
     local_xgram = jnp.dot(x_rows, x_rows.T, precision=precise, preferred_element_type=jnp.float32)
-    gram_x = lax.psum(local_xgram, ("gx", "gy"))
+    gram_x = local_xgram
+    for dev_j in ("gx", "gy"):
+        gram_x = lax.psum(gram_x, dev_j)
     column_count = y_cells * lax.axis_size("gy") * species * rank_kept
     x_triangle = jnp.linalg.cholesky(gram_x).T / jnp.sqrt(jnp.float32(column_count))
     return (core_tensor, z_basis, x_triangle)

time: 676 us -> 637 us (0.942)
  waiting for transfers between devices: 501 us -> 463 us
    psum x1 -> x2, waiting for transfers between devices: 248 us -> 210 us  [local(): gram_x = lax.psum(gram_x, dev_j)]
  transfers between devices with their start and end apart: 2 -> 3, of which waited for: 2 -> 3; matrix products, arithmetic and copies ran while one was open for 0% -> 0% of each run, Pallas kernels for 0% -> 0%
where the time goes in v2:
time: 637 us
  waiting for transfers between devices  463 us (73%)
  other arithmetic  78.3 us (12%)
  matrix products  36.2 us (6%)
  local copies, waits for them, and re-layouts  24.3 us (4%)
  blocking collectives  19.2 us (3%)
  between operations  15.4 us (2%)
    psum x1, waiting for transfers between devices, local(): gram_z = lax.psum(local_gram, ('gx', 'gy'))  253 us
    psum x2, waiting for transfers between devices, local(): gram_x = lax.psum(gram_x, dev_j)  210 us
    another operation x6, other arithmetic, local(): jnp.linalg.cholesky(gram_x).T / jnp.sqrt(jnp.float32(column_count))  34 us
    another operation x18, other arithmetic, orthonormal(): lower_factor = jnp.linalg.cholesky(inner_gram)  21.6 us
    all_to_all x1, blocking collectives, local(): lax.all_to_all(core_tensor, 'gx', split_axis=2, concat_axis=0, tiled=True)  19.2 us
    another operation x12, other arithmetic, orthonormal(): lax.linalg.triangular_solve(lower_factor, image, left_side=False, lower=T...  18.5 us
    dot_general x1, matrix products, local(): lax.dot_general(unfolded, unfolded, (((0,), (0,)), ((), ())), precision=p...  17.8 us
  transfers between devices with their start and end apart: 3, of which 3 were waited for; matrix products, arithmetic and copies ran while one was open for 0% of the time, Pallas kernels for 0%

profile of v2, /device:TPU:2, one launch (start us, length us, event | category | flops | bytes accessed | tf_op | source)
XLA Modules:
  0.0 636.9 jit_solution(13221397648058610220)
XLA Ops:
  7.2 17.8 %convolution_bitcast_fusion.1 = f32[256,256]{1,0:T(8,128)} fusion(f32[32,16,16,256]{3,2,1,0:T(8,128)} %param.5), kind=kOutput, calls=%fused_computation.1 | convolution fusion | flops 6442450944 | bytes 8650752 | tf_op jit(solution)/shard_map/dot_general | solution.py:23
  25.3 253.2 %all-reduce.5.cloned.1.call-done = f32[256,256]{1,0:T(8,128)} async-done(((f32[256,256]{1,0:T(8,128)}), f32[256,256]{1,0:T(8,128)}) %all-reduce.5.cloned.1.call-update) | async-done | bytes 262160 | tf_op jit(solution)/shard_map/psum | solution.py:31
  278.4 1.3 fusion.32
  280.0 2.9 cholesky.222
  284.2 2.4 custom-call.22
  287.2 2.9 cholesky.233
  291.4 2.4 custom-call.23
  294.1 1.3 fusion.35
  295.7 2.9 cholesky.244
  299.9 2.4 custom-call.24
  302.9 2.9 cholesky.255
  307.1 2.4 custom-call.25
  309.8 1.3 fusion.38
  311.3 2.9 cholesky.266
  315.6 2.4 custom-call.26
  318.5 2.9 cholesky.277
  322.8 2.4 custom-call.27
  325.5 9.9 %convolution_bitcast_fusion = f32[8192,32]{0,1:T(8,128)S(1)} fusion(f32[256,32]{0,1:T(8,128)S(1)} %convolution_bitcast_fusion.2, f32[8192,256]{1,0:T(8,128)} %bitcast.127), kind=kOutput, calls=%fused_computation | convolution fusion | flops 805306368 | bytes 9469952 | tf_op jit(solution)/shard_map/dot_general | solution.py:37
  335.4 2.6 copy.47
  338.0 3.5 reshape.41
  341.6 3.8 copy.48
  345.4 3.9 reshape.66
  349.3 19.2 %all_to_all.15 = f32[8,1,32768]{2,1,0:T(1,128)S(1)} all-to-all(f32[8,1,32768]{2,1,0:T(1,128)S(1)} %reshape.66), channel_id=1, replica_groups=mesh['gx'=8,'gy'=32] {'gx'}, dimensions={0} | all-to-all | bytes 2097152 | tf_op jit(solution)/shard_map/all_to_all | solution.py:40
  369.1 3.1 reduce.16
  372.2 3.3 reshape.67
  375.5 3.6 copy.49
  379.7 1.7 fusion.41
  381.8 60.3 %all-reduce.7.cloned.1.call-done = f32[256,256]{0,1:T(8,128)} async-done(((f32[256,256]{0,1:T(8,128)}), f32[256,256]{0,1:T(8,128)}) %all-reduce.7.cloned.1.call-update) | async-done | bytes 262160 | tf_op jit(solution)/shard_map/psum | solution.py:45
  442.1 149.4 %all-reduce.9.cloned.1.call-done = f32[256,256]{0,1:T(8,128)} async-done(((f32[256,256]{0,1:T(8,128)}), f32[256,256]{0,1:T(8,128)}) %all-reduce.9.cloned.1.call-update) | async-done | bytes 262160 | tf_op jit(solution)/shard_map/psum | solution.py:45
  593.6 11.7 %cholesky.77 = f32[128,128]{1,0:T(8,128)S(1)} custom-call(f32[128,128]{1,0:T(8,128)S(1)} %cholesky.286), custom_call_target="Cholesky" | custom-call | tf_op jit(solution)/shard_map/jit(cholesky)/cholesky | solution.py:47
  605.4 9.8 %custom-call.16 = f32[1,128,128]{1,2,0:T(8,128)S(1)} custom-call(f32[1,128,128]{2,1,0:T(8,128)S(1)} %get-tuple-element.20), custom_call_target="InvertDiagBlocksLowerTriangular" | custom-call | tf_op jit(solution)/shard_map/jit(cholesky)/cholesky | solution.py:47
  615.7 11.7 %cholesky.132 = f32[128,128]{1,0:T(8,128)S(1)} custom-call(f32[128,128]{1,0:T(8,128)S(1)} %convolution_subtract_fusion), custom_call_target="Cholesky" | custom-call | tf_op jit(solution)/shard_map/jit(cholesky)/cholesky | solution.py:47
  (67 shorter events, 16.8 us)
Async XLA Ops:
  7.2 271.3 %copy-start = (f32[256,32]{0,1:T(8,128)S(1)}, f32[256,32]{0,1:T(8,128)}, u32[]{:S(2)}) copy-start(f32[256,32]{0,1:T(8,128)} %param.6) | copy-start | bytes 98308
  7.2 271.2 %all-reduce.5.cloned.1.call-start = ((), (), s32[]{:S(2)}) async-start(), calls=%async_computation.1 | async-start | bytes 524288 | tf_op jit(solution)/shard_map/psum | solution.py:31
  25.0 417.1 %all-reduce.7.cloned.1.call-start = ((), (), s32[]{:S(2)}) async-start(), calls=%async_computation.2 | async-start | bytes 524288 | tf_op jit(solution)/shard_map/psum | solution.py:45
  325.5 16.1 %copy-start.2 = (f32[256,32]{0,1:T(8,128)}, f32[256,32]{0,1:T(8,128)S(1)}, u32[]{:S(2)}) copy-start(f32[256,32]{0,1:T(8,128)S(1)} %convolution_bitcast_fusion.2) | copy-start | bytes 98308
  341.6 34.0 %copy-start.1 = (f32[32,16,512]{2,1,0:T(8,128)}, f32[32,16,512]{2,1,0:T(8,128)S(1)}, u32[]{:S(2)}) copy-start(f32[32,16,512]{2,1,0:T(8,128)S(1)} %reshape.41) | copy-start | bytes 3145732
  381.5 210.1 %all-reduce.9.cloned.1.call-start = ((), (), s32[]{:S(2)}) async-start(), calls=%async_computation.3 | async-start | bytes 524288 | tf_op jit(solution)/shard_map/psum | solution.py:45
Sparse Core Ops, SparseCore 0:
  25.2 253.2 all-reduce.4
  381.6 60.4 all-reduce.6
  446.0 145.5 all-reduce.8
